TPU v7x, 32 devices: a whole 2x2x4 slice. The times are simulated.
32 devices in a mesh: groups: 2 (over y), cuts: 4 (over z), mesh: 2 (over x), sub: 2 (over core).
Axes of the slice: x: 2, y: 2, z: 4, core: 2. Of those that a mesh axis runs over, the one named last changes fastest.
Arguments:
- couplings: float32 [64, 64, 256], P(('mesh', 'sub')), may hold values from 0 to 0.004464286
- edge_mask: int32 [64, 3], P(('mesh', 'sub')), may hold values 0 or 1
- slice_mass: float32 [8, 4096], P(('groups', 'cuts'), ('mesh', 'sub')), parts along dimension 0, may hold values from 0.003 to 700
- sources: float32 [8, 2, 4096], P(('groups', 'cuts'), None, ('mesh', 'sub')), parts along dimension 0, may hold values from -20 to 20
- slice_states: float32 [8, 4096], P(('groups', 'cuts'), ('mesh', 'sub')), parts along dimension 0, may hold values from -6 to 6
Outputs:
- new_states: float32 [8, 4096], P(('groups', 'cuts'), ('mesh', 'sub')), parts along dimension 0
- defect: float32 [8, 4096], P(('groups', 'cuts'), ('mesh', 'sub')), parts along dimension 0
There are 2 independent parts, one for each index of `groups`. A program takes and returns all parts, laid end to end along the dimension named above; an argument that names none is the same for every part. Nothing has to cross between parts.
All inputs are finite; a program needn't handle non-finite values. No bound on the sum of `edge_mask` on one device may be relied on, other than what follows from the above.
Results may differ from a plain program's by a relative error of at most 0.0003.
Values sent between devices are 32-bit elements; how exact they have to be, the bound alone decides.
A program may use at most 64 MiB of HBM per device.

v0:
```python
import functools

import jax
import jax.numpy as jnp
from jax import lax
from jax.experimental import pallas as pl
from jax.experimental.pallas import tpu as pltpu
from jax.sharding import PartitionSpec as P

REACH = 3
CG_ITERS = 4
SWEEPS = 2
BLOCK = 64
LANES = 128
ROWS = 8
HALO = 2 * LANES
MESH = pl.DeviceIdType.MESH


def kernel(sizes, coup, mask, mass_ref, src_ref, st_ref, new_ref, def_ref,
           W, hsend, hrecv, vsend, vrecv, send, recv, csend, crecv, spread,
           hsem, vsem, xs_sem, xr_sem, cs_sem, cr_sem):
    n_mesh, n_sub, n_cut = sizes
    n_sec = n_mesh * n_sub
    blocks = coup.shape[0]
    groups = blocks // 2
    local = blocks * BLOCK
    wide = local + 2 * HALO
    tiles = wide // LANES
    steps = src_ref.shape[1]

    sector = lax.axis_index("mesh") * n_sub + lax.axis_index("sub")
    cut = lax.axis_index("cuts")

    def sector_id(distance):
        other = lax.rem(sector + distance, n_sec)
        return {"mesh": other // n_sub, "sub": lax.rem(other, n_sub)}

    def cut_id(distance):
        return {"cuts": lax.rem(cut + distance, n_cut)}

    barrier = pltpu.get_barrier_semaphore()
    for d in range(1, n_sec):
        pl.semaphore_signal(barrier, inc=1, device_id=sector_id(d), device_id_type=MESH)
    for d in range(1, n_cut):
        pl.semaphore_signal(barrier, inc=1, device_id=cut_id(d), device_id_type=MESH)

    low_half = lax.broadcasted_iota(jnp.int32, (BLOCK, LANES), 1) < BLOCK
    low_row = lax.broadcasted_iota(jnp.int32, (ROWS, LANES), 1) < BLOCK
    row = lax.broadcasted_iota(jnp.int32, (ROWS, LANES), 0)

    def factors(b):
        return [mask[b, k].astype(jnp.float32) for k in range(REACH)]

    def masked(b):
        m = factors(b)
        near = coup[b, :, :LANES] * jnp.where(low_half, 1.0, m[0])
        far = coup[b, :, LANES:] * jnp.where(low_half, m[1], m[2])
        return near, far

    def turned(x):
        return pltpu.roll(x, BLOCK, 1)

    near1, far1 = masked(blocks - 1)
    _, far2 = masked(blocks - 2)
    _, far3 = masked(blocks - 3)
    near1t, far1t, far3t = turned(near1), turned(far1), turned(far3)
    hsend[0] = jnp.where(low_half, near1t, far1t)
    hsend[1] = far2
    hsend[2] = jnp.where(low_half, far3t, far1)
    for i, at in enumerate((local - HALO, 0)):
        vsend[i, 0:1, :] = mass_ref[0:1, at:at + HALO]
        vsend[i, 1:2, :] = st_ref[0:1, at:at + HALO]
        for s in range(steps):
            vsend[i, 2 + s:3 + s, :] = src_ref[0, s:s + 1, at:at + HALO]

    pl.semaphore_wait(barrier, n_sec - 1 + n_cut - 1)

    right, left = sector_id(1), sector_id(n_sec - 1)
    first = [
        pltpu.make_async_remote_copy(hsend, hrecv, hsem.at[0], hsem.at[1], device_id=right, device_id_type=MESH),
        pltpu.make_async_remote_copy(vsend.at[0], vrecv.at[0], vsem.at[0], vsem.at[1], device_id=right, device_id_type=MESH),
        pltpu.make_async_remote_copy(vsend.at[1], vrecv.at[1], vsem.at[2], vsem.at[3], device_id=left, device_id_type=MESH),
    ]
    for copy in first:
        copy.start()

    def put(g, at, block):
        high = block.astype(jnp.bfloat16)
        low = (block - high.astype(jnp.float32)).astype(jnp.bfloat16)
        W[g, at * BLOCK:(at + 1) * BLOCK, :LANES] = high
        W[g, at * BLOCK:(at + 1) * BLOCK, LANES:] = low

    unit = lax.broadcasted_iota(jnp.int32, (BLOCK, LANES), 0) == lax.rem(
        lax.broadcasted_iota(jnp.int32, (BLOCK, LANES), 1), BLOCK)
    zero = jnp.zeros((BLOCK, LANES), jnp.float32)
    for g in range(groups):
        n0, f0 = masked(2 * g)
        n1, f1 = masked(2 * g + 1)
        near_t = jnp.concatenate([n0, n1], axis=0).T
        far_t = jnp.concatenate([f0, f1], axis=0).T
        own_t, k1_t = near_t[:BLOCK], near_t[BLOCK:]
        k2_t, k3_t = far_t[:BLOCK], far_t[BLOCK:]
        n1t, f1t = turned(n1), turned(f1)
        put(g, 4, jnp.where(low_half, jnp.where(unit, 0.0, 0.5 * (n0 + own_t)), n0))
        put(g, 5, jnp.where(low_half, k1_t, jnp.where(unit, 0.0, 0.5 * (n1t + own_t))))
        put(g, 6, jnp.where(low_half, k2_t, k1_t))
        put(g, 7, jnp.where(low_half, k3_t, k2_t))
        put(g, 0, jnp.where(low_half, zero, k3_t))
        if g + 1 < groups:
            put(g + 1, 2, f0)
            put(g + 1, 3, jnp.where(low_half, n1t, f1t))
        if g + 2 < groups:
            put(g + 2, 1, jnp.where(low_half, f1t, zero))

    for copy in first:
        copy.wait()
    put(0, 3, hrecv[0])
    put(0, 2, hrecv[1])
    z = hrecv[2]
    put(0, 1, jnp.where(low_half, z, zero))
    put(1, 1, jnp.where(low_half, turned(z), zero))

    def spanned(at, middle):
        whole = jnp.concatenate([vrecv[0, at:at + 1, :], middle, vrecv[1, at:at + 1, :]], axis=1)
        return jnp.broadcast_to(whole, (ROWS, wide))

    def total(x):
        x = x + pltpu.roll(x, 4, 0)
        x = x + pltpu.roll(x, 2, 0)
        return x + pltpu.roll(x, 1, 0)

    row_wide = lax.broadcasted_iota(jnp.int32, (ROWS, wide), 0)

    def coupled(v):
        h = v.astype(jnp.bfloat16).astype(jnp.float32)
        rest = v - h
        m = rest.astype(jnp.bfloat16).astype(jnp.float32)
        parts = jnp.where(row_wide == 0, h, jnp.where(row_wide == 1, m, jnp.where(row_wide == 2, rest - m, 0.0)))
        cast = parts.astype(jnp.bfloat16)
        out = []
        for g in range(groups):
            at = g * LANES
            ends = jnp.where(low_row, parts[:, at + 4 * LANES:at + 5 * LANES], parts[:, at:at + LANES])
            lhs = jnp.concatenate([ends.astype(jnp.bfloat16), cast[:, at + LANES:at + 4 * LANES]], axis=1)
            r = jnp.dot(lhs, W[g], preferred_element_type=jnp.float32)
            out.append(total(r[:, :LANES] + r[:, LANES:]))
        return jnp.concatenate(out, axis=1)

    def stacked(*values):
        message = values[-1]
        for i in range(len(values) - 2, -1, -1):
            message = jnp.where(row == i, values[i], message)
        return message

    def folded(x):
        parts = [x[:, i * LANES:(i + 1) * LANES] for i in range(groups)]
        while len(parts) > 1:
            parts = [sum(parts[i:i + 2]) for i in range(0, len(parts), 2)]
        return parts[0]

    def exchange(slot, w, rr, rw, sums):
        end = local - HALO
        send[slot, 0] = stacked(w[:, end:end + LANES], w[:, end + LANES:], rr, rw,
                                sums[:, end:end + LANES], sums[:, end + LANES:])
        send[slot, 1] = stacked(w[:, :LANES], w[:, LANES:HALO], rr, rw,
                                sums[:, :LANES], sums[:, LANES:HALO])
        copies = []
        for d in range(1, n_sec):
            copies.append(pltpu.make_async_remote_copy(
                send.at[slot, 1 if d == n_sec - 1 else 0], recv.at[slot, d - 1],
                xs_sem.at[slot, d - 1], xr_sem.at[slot, d - 1],
                device_id=sector_id(d), device_id_type=MESH))
        for copy in copies:
            copy.start()
        for copy in copies:
            copy.wait()

        def line(d, i):
            return jnp.broadcast_to(recv[slot, d - 1, i:i + 1, :], (ROWS, LANES))

        for d in range(1, n_sec):
            rr = rr + line(d, 2)
            rw = rw + line(d, 3)
        w = jnp.concatenate([line(1, 0), line(1, 1), w, line(n_sec - 1, 0), line(n_sec - 1, 1)], axis=1)
        return w, jnp.sum(rr, axis=1, keepdims=True), jnp.sum(rw, axis=1, keepdims=True)

    mass = spanned(0, mass_ref[...])
    states = spanned(1, st_ref[...])
    sums = coupled(jnp.ones((ROWS, wide), jnp.float32))
    diagonal = mass[:, HALO:HALO + local] + sums

    def solve(rhs):
        r = rhs
        x = p = s = alpha = old = None
        for it in range(CG_ITERS):
            mine = r[:, HALO:HALO + local]
            w = diagonal * mine - coupled(r)
            w, rr, rw = exchange(it % 2, w, folded(mine * mine), folded(mine * w), sums)
            if it == 0:
                alpha = rr / rw
                p, s = r, w
                x = alpha * p
            else:
                beta = rr / old
                alpha = rr / (rw - beta * rr / alpha)
                p, s = r + beta * p, w + beta * s
                x = x + alpha * p
            if it + 1 < CG_ITERS:
                r = r - alpha * s
            old = rr
        return x

    def to_rows(ref, x):
        for t in range(tiles):
            ref[t:t + 1, :] = x[0:1, t * LANES:(t + 1) * LANES]

    rate = None
    for sweep in range(SWEEPS):
        def section(i, current):
            source = jnp.concatenate(
                [vrecv[0, pl.ds(2 + i, 1), :], src_ref[0, pl.ds(i, 1), :], vrecv[1, pl.ds(2 + i, 1), :]], axis=1)
            return solve(mass * current + jnp.broadcast_to(source, (ROWS, wide)))

        fine = lax.fori_loop(0, steps, section, states)
        if sweep == 0:
            slot = CG_ITERS - 1 - (CG_ITERS - 1) // 2 * 2
            edge = [jnp.broadcast_to(recv[slot, d, i:i + 1, :], (ROWS, LANES))
                    for d in (0, n_sec - 2) for i in (4, 5)]
            all_sums = jnp.concatenate([edge[0], edge[1], sums, edge[2], edge[3]], axis=1)
            rate = mass / (mass + steps * all_sums)
        offset = fine - rate * states
        to_rows(csend.at[sweep, 0], offset)
        to_rows(csend.at[sweep, 1], rate if sweep == 0 else fine)
        copies = [pltpu.make_async_remote_copy(
            csend.at[sweep], crecv.at[sweep, cut], cs_sem.at[sweep, d - 1], cr_sem.at[sweep, d - 1],
            device_id=cut_id(d), device_id_type=MESH) for d in range(1, n_cut)]
        for copy in copies:
            copy.start()
        crecv[sweep, cut] = csend[sweep]
        for copy in copies:
            copy.wait()
        p_run = jnp.ones((tiles, LANES), jnp.float32)
        q_run = jnp.zeros((tiles, LANES), jnp.float32)
        p_mine, q_mine = p_run, q_run
        for j in range(n_cut):
            here = cut == j
            p_mine = jnp.where(here, p_run, p_mine)
            q_mine = jnp.where(here, q_run, q_mine)
            a = crecv[0, j, 1, :tiles]
            b = crecv[sweep, j, 0, :tiles]
            p_run, q_run = a * p_run, a * q_run + b
        new = p_mine * (q_run / (1.0 - p_run)) + q_mine
        if sweep == SWEEPS - 1:
            arrived = crecv[sweep, lax.rem(cut + n_cut - 1, n_cut), 1, :tiles]
            spread[:tiles, :] = arrived
            for t in range(2, tiles - 2):
                at = (t - 2) * LANES
                def_ref[0:1, at:at + LANES] = spread[t:t + 1, :] - states[0:1, t * LANES:(t + 1) * LANES]
                new_ref[0:1, at:at + LANES] = new[t:t + 1, :]
        else:
            spread[:tiles, :] = new
            states = jnp.concatenate(
                [jnp.broadcast_to(spread[t:t + 1, :], (ROWS, LANES)) for t in range(tiles)], axis=1)


def shards(sizes, couplings, edge_mask, slice_mass, sources, slice_states):
    n_mesh, n_sub, n_cut = sizes
    n_sec = n_mesh * n_sub
    blocks = couplings.shape[0]
    wide = blocks * BLOCK + 2 * HALO
    tiles = wide // LANES
    lines = -(-tiles // ROWS) * ROWS
    steps = sources.shape[1]
    vrows = -(-(2 + steps) // ROWS) * ROWS
    f32 = jnp.float32
    vmem = pl.BlockSpec(memory_space=pltpu.VMEM)
    out = jax.ShapeDtypeStruct(slice_states.shape, f32)
    return pl.pallas_call(
        functools.partial(kernel, sizes),
        out_shape=(out, out),
        in_specs=[vmem, pl.BlockSpec(memory_space=pltpu.SMEM), vmem, vmem, vmem],
        out_specs=(vmem, vmem),
        scratch_shapes=[
            pltpu.VMEM((blocks // 2, 8 * BLOCK, 2 * LANES), jnp.bfloat16),
            pltpu.VMEM((3, BLOCK, LANES), f32),
            pltpu.VMEM((3, BLOCK, LANES), f32),
            pltpu.VMEM((2, vrows, HALO), f32),
            pltpu.VMEM((2, vrows, HALO), f32),
            pltpu.VMEM((2, 2, ROWS, LANES), f32),
            pltpu.VMEM((2, n_sec - 1, ROWS, LANES), f32),
            pltpu.VMEM((SWEEPS, 2, lines, LANES), f32),
            pltpu.VMEM((SWEEPS, n_cut, 2, lines, LANES), f32),
            pltpu.VMEM((lines, LANES), f32),
            pltpu.SemaphoreType.DMA((2,)),
            pltpu.SemaphoreType.DMA((4,)),
            pltpu.SemaphoreType.DMA((2, n_sec - 1)),
            pltpu.SemaphoreType.DMA((2, n_sec - 1)),
            pltpu.SemaphoreType.DMA((SWEEPS, n_cut - 1)),
            pltpu.SemaphoreType.DMA((SWEEPS, n_cut - 1)),
        ],
        compiler_params=pltpu.CompilerParams(
            collective_id=0, has_side_effects=True, vmem_limit_bytes=32 * 1024 * 1024),
    )(couplings, edge_mask, slice_mass, sources, slice_states)


def solution(mesh):
    rows = P(("groups", "cuts"), ("mesh", "sub"))
    placed = (
        P(("mesh", "sub"), None, None),
        P(("mesh", "sub"), None),
        rows,
        P(("groups", "cuts"), None, ("mesh", "sub")),
        rows,
    )
    sizes = (mesh.shape["mesh"], mesh.shape["sub"], mesh.shape["cuts"])
    return jax.shard_map(
        functools.partial(shards, sizes),
        mesh=mesh,
        in_specs=placed,
        out_specs=(rows, rows),
        check_vma=False,
    )
```

profile of v0, /device:TPU:0, one launch (start us, length us, event | category | flops | bytes accessed | tf_op | source)
XLA Modules:
  0.0 71.6 jit_solution(5653375624108600850)
XLA Ops:
  0.6 0.0 copy-start.1
  0.6 0.8 %copy.7.mask = s32[16,3]{1,0:T(8,128)S(1)} copy(s32[16,3]{0,1:T(4,128)} %param.6) | data formatting | bytes 384 | tf_op args[1]
  1.4 0.0 copy-done.1
  1.4 0.0 copy-start
  1.4 1.2 %copy-done = f32[16,64,256]{2,1,0:T(8,128)S(1)} copy-done((f32[16,64,256]{2,1,0:T(8,128)S(1)}, f32[16,64,256]{2,1,0:T(8,128)}, u32[]{:S(2)}) %copy-start) | copy-done | bytes 1048600
  2.6 0.0 copy-start.2
  2.6 0.7 copy-done.2
  3.3 0.0 copy-start.3
  3.3 0.7 copy-done.3
  4.0 66.4 %shard_map.68 = (f32[1,1024]{1,0:T(1,128)S(1)}, f32[1,1024]{1,0:T(1,128)S(1)}) custom-call(f32[16,64,256]{2,1,0:T(8,128)S(1)} %copy-done, s32[16,3]{1,0:T(8,128)S(1)} %copy.7.mask, f32[1,1024]{1,0:T(1,128)S(1)} %copy-done.2, f32[1,2,1024]{2,1,0:T(2,128)S(1)} %copy-done.1, f32[1,1024]{1,0:T(1,128)S(1)} %copy-done.3), custom_call_target="tpu_custom_call" | custom-call | tf_op jit(solution)/shard_map/pallas_call | solution.py:279
  70.5 0.6 copy.10
  71.1 0.6 copy.11
Async XLA Ops:
  0.6 0.8 %copy-start.1 = (f32[1,2,1024]{2,1,0:T(2,128)S(1)}, f32[1,2,1024]{2,1,0:T(2,128)}, u32[]{:S(2)}) copy-start(f32[1,2,1024]{2,1,0:T(2,128)} %src_ref.1) | copy-start | bytes 24580
  1.4 1.2 %copy-start = (f32[16,64,256]{2,1,0:T(8,128)S(1)}, f32[16,64,256]{2,1,0:T(8,128)}, u32[]{:S(2)}) copy-start(f32[16,64,256]{2,1,0:T(8,128)} %coup.1) | copy-start | bytes 3145732
  2.6 0.7 copy-start.2
  3.3 0.7 copy-start.3
where the time goes:
time: 71.9 us; the launch traced here: 71.6 us
  Pallas kernels  66.4 us (92%)
  local copies, waits for them, and re-layouts  4.55 us (6%)
    pallas_call x1, Pallas kernels, shards(): pl.pallas_call(functools.partial(kernel, sizes), out_shape=(out, out), in...  66.4 us
    unnamed x11, local copies, waits for them, and re-layouts  4.55 us

commit v1 on v0

v1 whole, which is shorter than its diff:
```python
import functools

import jax
import jax.numpy as jnp
from jax import lax
from jax.experimental import pallas as pl
from jax.experimental.pallas import tpu as pltpu
from jax.sharding import PartitionSpec as P

REACH = 3
CG_ITERS = 4
SWEEPS = 2
BLOCK = 64
LANES = 128
ROWS = 8
HALO = 3 * LANES
BEFORE = 2 * REACH
MESH = pl.DeviceIdType.MESH


def kernel(sizes, coup, mask, mass_ref, src_ref, st_ref, new_ref, def_ref,
           W, ext, fac, vsend, vrecv, tsend, trecv, send, recv, csend, crecv, spread,
           lsem, hsem, fsem, vsem, ts_sem, tr_sem, xs_sem, xr_sem, cs_sem, cr_sem):
    n_mesh, n_sub, n_cut = sizes
    n_sec = n_mesh * n_sub
    blocks = coup.shape[0]
    groups = blocks // 2
    local = blocks * BLOCK
    wide = local + 2 * HALO
    tiles = wide // LANES
    edge = HALO // LANES
    steps = src_ref.shape[1]

    sector = lax.axis_index("mesh") * n_sub + lax.axis_index("sub")
    cut = lax.axis_index("cuts")

    def sector_id(distance):
        other = lax.rem(sector + distance, n_sec)
        return {"mesh": other // n_sub, "sub": lax.rem(other, n_sub)}

    def cut_id(distance):
        return {"cuts": lax.rem(cut + distance, n_cut)}

    barrier = pltpu.get_barrier_semaphore()
    for d in range(1, n_sec):
        pl.semaphore_signal(barrier, inc=1, device_id=sector_id(d), device_id_type=MESH)
    for d in range(1, n_cut):
        pl.semaphore_signal(barrier, inc=1, device_id=cut_id(d), device_id_type=MESH)
    fetch = pltpu.make_async_copy(coup, ext.at[BEFORE:BEFORE + blocks], lsem)
    fetch.start()

    low_half = lax.broadcasted_iota(jnp.int32, (BLOCK, LANES), 1) < BLOCK
    low_row = lax.broadcasted_iota(jnp.int32, (ROWS, LANES), 1) < BLOCK
    low_line = lax.broadcasted_iota(jnp.int32, (1, LANES), 1) < BLOCK
    row = lax.broadcasted_iota(jnp.int32, (ROWS, LANES), 0)
    zero = jnp.zeros((BLOCK, LANES), jnp.float32)

    for b in range(blocks):
        m = [mask[k, b].astype(jnp.float32) for k in range(REACH)]
        fac[BEFORE + b, 0:1, :] = jnp.where(low_line, 1.0, m[0])
        fac[BEFORE + b, 1:2, :] = jnp.where(low_line, m[1], m[2])
    last = BEFORE + blocks + REACH
    fac[last] = jnp.zeros((2, LANES), jnp.float32)
    ext[last, :, :LANES] = zero
    ext[last, :, LANES:] = zero
    for b in range(2):
        ext[b, :, :LANES] = zero
    for i, at in enumerate((local - HALO, 0)):
        vsend[i, 0:1, :] = mass_ref[0:1, at:at + HALO]
        vsend[i, 1:2, :] = st_ref[0:1, at:at + HALO]
        for s in range(steps):
            vsend[i, 2 + s:3 + s, :] = src_ref[0, s:s + 1, at:at + HALO]

    def folded(x):
        parts = [x[:, i * LANES:(i + 1) * LANES] for i in range(x.shape[1] // LANES)]
        while len(parts) > 1:
            parts = [sum(parts[i:i + 2]) for i in range(0, len(parts), 2)]
        return parts[0]

    tsend[...] = jnp.broadcast_to(folded(mass_ref[...]), (ROWS, LANES))

    pl.semaphore_wait(barrier, n_sec - 1 + n_cut - 1)

    right, left = sector_id(1), sector_id(n_sec - 1)
    after = BEFORE + blocks

    def to(src, dst, sems, i, who):
        return pltpu.make_async_remote_copy(
            src, dst, sems.at[i], sems.at[i + 1], device_id=who, device_id_type=MESH)

    first = [
        to(coup.at[blocks - 4:blocks], ext.at[2:BEFORE], hsem, 0, right),
        to(coup.at[0:REACH], ext.at[after:last], hsem, 2, left),
        to(coup.at[blocks - BEFORE:blocks - 4, :, LANES:], ext.at[0:2, :, LANES:], hsem, 4, right),
        to(fac.at[blocks:after], fac.at[0:BEFORE], fsem, 0, right),
        to(fac.at[BEFORE:BEFORE + REACH], fac.at[after:last], fsem, 2, left),
        to(vsend.at[0], vrecv.at[0], vsem, 0, right),
        to(vsend.at[1], vrecv.at[1], vsem, 2, left),
    ]
    for d in range(1, n_sec):
        first.append(pltpu.make_async_remote_copy(
            tsend, trecv.at[d - 1], ts_sem.at[d - 1], tr_sem.at[d - 1],
            device_id=sector_id(d), device_id_type=MESH))
    for copy in first[3:] + first[:3]:
        copy.start()

    def turned(x):
        return pltpu.roll(x, BLOCK, 1)

    n_w = groups + 4

    def put(g, at, block):
        if not 0 <= g < n_w:
            return
        high = block.astype(jnp.bfloat16)
        low = (block - high.astype(jnp.float32)).astype(jnp.bfloat16)
        W[g, at * BLOCK:(at + 1) * BLOCK, :LANES] = high
        W[g, at * BLOCK:(at + 1) * BLOCK, LANES:] = low

    unit = lax.broadcasted_iota(jnp.int32, (BLOCK, LANES), 0) == lax.rem(
        lax.broadcasted_iota(jnp.int32, (BLOCK, LANES), 1), BLOCK)

    def masked(b):
        return ext[b, :, :LANES] * fac[b, 0:1, :], ext[b, :, LANES:] * fac[b, 1:2, :]

    def build(pair):
        g = pair + 2
        n0, f0 = masked(2 * pair + BEFORE)
        n1, f1 = masked(2 * pair + BEFORE + 1)
        n1t, f1t = turned(n1), turned(f1)
        put(g + 1, 2, f0)
        put(g + 1, 3, jnp.where(low_half, n1t, f1t))
        put(g + 2, 1, jnp.where(low_half, f1t, zero))
        if g < 0:
            return
        near_t = jnp.concatenate([n0, n1], axis=0).T
        far_t = jnp.concatenate([f0, f1], axis=0).T
        own_t, k1_t = near_t[:BLOCK], near_t[BLOCK:]
        k2_t, k3_t = far_t[:BLOCK], far_t[BLOCK:]
        put(g, 4, jnp.where(low_half, jnp.where(unit, 0.0, 0.5 * (n0 + own_t)), n0))
        put(g, 5, jnp.where(low_half, k1_t, jnp.where(unit, 0.0, 0.5 * (n1t + own_t))))
        put(g, 6, jnp.where(low_half, k2_t, k1_t))
        put(g, 7, jnp.where(low_half, k3_t, k2_t))
        put(g, 0, jnp.where(low_half, zero, k3_t))

    put(0, 1, zero)
    fetch.wait()
    for pair in range(groups):
        build(pair)
    for copy in first:
        copy.wait()
    for pair in (-3, -2, -1, groups, groups + 1):
        build(pair)

    def spanned(at, middle):
        whole = jnp.concatenate([vrecv[0, at:at + 1, :], middle, vrecv[1, at:at + 1, :]], axis=1)
        return jnp.broadcast_to(whole, (ROWS, wide))

    def total(x):
        x = x + pltpu.roll(x, 4, 0)
        x = x + pltpu.roll(x, 2, 0)
        return x + pltpu.roll(x, 1, 0)

    def tile(x, i):
        return x[:, i * LANES:(i + 1) * LANES]

    def coupled(vectors, begin, count):
        width = vectors[0].shape[1]
        rows = lax.broadcasted_iota(jnp.int32, (ROWS, width), 0)
        parts = jnp.zeros((ROWS, width), jnp.float32)
        for i, v in enumerate(vectors):
            h = v.astype(jnp.bfloat16).astype(jnp.float32)
            rest = v - h
            m = rest.astype(jnp.bfloat16).astype(jnp.float32)
            for j, part in enumerate((h, m, rest - m)):
                parts = jnp.where(rows == 3 * i + j, part, parts)
        cast = parts.astype(jnp.bfloat16)
        blank = jnp.zeros((ROWS, LANES), jnp.float32)
        n_tiles = width // LANES
        out = [[] for _ in vectors]
        for t in range(count):
            centre = t + begin
            up = tile(parts, centre + 2) if centre + 2 < n_tiles else blank
            down = tile(parts, centre - 2) if centre >= 2 else blank
            ends = jnp.where(low_row, up, down).astype(jnp.bfloat16)
            lhs = jnp.concatenate([ends, cast[:, (centre - 1) * LANES:(centre + 2) * LANES]], axis=1)
            g = t + (n_w - count) // 2
            r = jnp.dot(lhs, W[g], preferred_element_type=jnp.float32)
            r = r[:, :LANES] + r[:, LANES:]
            if len(vectors) == 1:
                out[0].append(total(r))
            else:
                out[0].append(total(jnp.where(row < 3, r, 0.0)))
                out[1].append(total(jnp.where(row < 3, 0.0, r)))
        return [jnp.concatenate(o, axis=1) for o in out]

    def stacked(values):
        halves = []
        for at in (0, ROWS):
            message = jnp.zeros((ROWS, LANES), jnp.float32)
            for i in range(ROWS):
                if at + i in values:
                    message = jnp.where(row == i, values[at + i], message)
            halves.append(message)
        return jnp.concatenate(halves, axis=0)

    def exchange(slot, dots, rims):
        ends = []
        for side in range(2):
            values = dict(enumerate(dots))
            for at, v in rims:
                for i in range(edge):
                    values[at + i] = tile(v, i if side else groups - edge + i)
            ends.append(stacked(values))
            send[slot, side] = ends[side]
        copies = []
        for d in range(1, n_sec):
            copies.append(pltpu.make_async_remote_copy(
                send.at[slot, 1 if d == n_sec - 1 else 0], recv.at[slot, d - 1],
                xs_sem.at[slot, d - 1], xr_sem.at[slot, d - 1],
                device_id=sector_id(d), device_id_type=MESH))
        for copy in copies:
            copy.start()
        for copy in copies:
            copy.wait()
        sums = ends[0]
        for d in range(1, n_sec):
            sums = sums + recv[slot, d - 1]
        sums = jnp.sum(sums, axis=1, keepdims=True)
        return [sums[i:i + 1, :] for i in range(len(dots))]

    def lined(slot, at, v):
        def line(d, i):
            return jnp.broadcast_to(recv[slot, d - 1, at + i:at + i + 1, :], (ROWS, LANES))
        return jnp.concatenate(
            [line(1, i) for i in range(edge)] + [v] + [line(n_sec - 1, i) for i in range(edge)], axis=1)

    def inner(x):
        return x[:, HALO:HALO + local]

    mass = spanned(0, mass_ref[...])
    states = spanned(1, st_ref[...])
    mean = tsend[...]
    for d in range(1, n_sec):
        mean = mean + trecv[d - 1]
    mean = jnp.sum(mean[0:1, :], axis=1, keepdims=True) * (1.0 / (n_sec * local))
    more = coupled([jnp.ones((ROWS, wide), jnp.float32)], 1, n_w)[0]
    sums = more[:, 2 * LANES:2 * LANES + local]
    outer = mass[:, LANES:wide - LANES] - mean + more
    core = inner(mass) - mean + sums

    def limited(step):
        return jnp.minimum(jnp.maximum(step, 1.0 / 710.0), 1.0 / 0.0029)

    def solve(rhs):
        r = rhs
        u = outer * r[:, LANES:wide - LANES] - coupled([r], 1, n_w)[0]
        u1 = u[:, 2 * LANES:2 * LANES + local]
        u2 = core * u1 - coupled([u], 2, groups)[0]
        r_in = inner(r)
        m0, m1, m2, m3 = exchange(
            0, [folded(r_in * r_in), folded(r_in * u1), folded(u1 * u1), folded(u1 * u2)],
            [(10, u1), (13, u2)])
        step = m0 / (m1 + mean * m0)
        keep = m1 / (m1 + mean * m0)
        rr = jnp.maximum(step * step * (m2 - m1 * (m1 / m0)), 1e-12 * m0)
        rb = keep * keep * m1 - 2.0 * keep * step * m2 + step * step * m3
        beta = rr / m0
        following = limited(rr / (rb + mean * rr - beta * (rr / step)))
        u1, u2 = lined(0, 10, u1), lined(0, 13, u2)
        r1 = keep * r - step * u1
        p = r1 + beta * r
        s = keep * u1 - step * u2 + beta * u1 + mean * p
        x = step * r + following * p
        r = r1 - following * s
        u = outer * r[:, LANES:wide - LANES] - coupled([r], 1, n_w)[0]
        u1 = u[:, 2 * LANES:2 * LANES + local]
        nu, ns = coupled([u, s[:, LANES:wide - LANES]], 2, groups)
        r_in, p_in, s_in = inner(r), inner(p), inner(s)
        u2, bs = core * u1 - nu, core * s_in - ns
        m0, m1, m2, m3, rs, ps, us, ss, sb, vs = exchange(
            1, [folded(a * b) for a, b in (
                (r_in, r_in), (r_in, u1), (u1, u1), (u1, u2), (r_in, s_in),
                (p_in, s_in), (u1, s_in), (s_in, s_in), (s_in, bs), (u2, s_in))],
            [(10, u1), (13, sums)])
        beta = -rs / ps
        step = limited(m0 / (m1 + mean * m0 + beta * rs))
        keep, c = 1.0 - mean * step, step * beta
        rr = (keep * keep * m0 + step * step * m2 + c * c * ss
              - 2.0 * keep * step * m1 - 2.0 * keep * c * rs + 2.0 * step * c * us)
        rr = jnp.maximum(rr, 1e-12 * m0)
        rb = (keep * keep * m1 + step * step * m3 + c * c * sb
              - 2.0 * keep * step * m2 - 2.0 * keep * c * us + 2.0 * step * c * vs)
        later = rr / m0
        following = limited(rr / (rb + mean * rr - later * (rr / step)))
        u1 = lined(1, 10, u1)
        p = r + beta * p
        s = u1 + mean * r + beta * s
        r = r - step * s
        return x + step * p + following * (r + later * p)

    def to_rows(ref, x):
        for t in range(tiles):
            ref[t:t + 1, :] = x[0:1, t * LANES:(t + 1) * LANES]

    rate = None
    for sweep in range(SWEEPS):
        def section(i, current):
            source = jnp.concatenate(
                [vrecv[0, pl.ds(2 + i, 1), :], src_ref[0, pl.ds(i, 1), :], vrecv[1, pl.ds(2 + i, 1), :]], axis=1)
            return solve(mass * current + jnp.broadcast_to(source, (ROWS, wide)))

        fine = lax.fori_loop(0, steps, section, states)
        if sweep == 0:
            rate = mass / (mass + steps * lined(1, 13, sums))
        offset = fine - rate * states
        to_rows(csend.at[sweep, 0], offset)
        to_rows(csend.at[sweep, 1], rate if sweep == 0 else fine)
        copies = [pltpu.make_async_remote_copy(
            csend.at[sweep], crecv.at[sweep, cut], cs_sem.at[sweep, d - 1], cr_sem.at[sweep, d - 1],
            device_id=cut_id(d), device_id_type=MESH) for d in range(1, n_cut)]
        for copy in copies:
            copy.start()
        crecv[sweep, cut] = csend[sweep]
        for copy in copies:
            copy.wait()
        p_run = jnp.ones((tiles, LANES), jnp.float32)
        q_run = jnp.zeros((tiles, LANES), jnp.float32)
        p_mine, q_mine = p_run, q_run
        for j in range(n_cut):
            here = cut == j
            p_mine = jnp.where(here, p_run, p_mine)
            q_mine = jnp.where(here, q_run, q_mine)
            a = crecv[0, j, 1, :tiles]
            b = crecv[sweep, j, 0, :tiles]
            p_run, q_run = a * p_run, a * q_run + b
        new = p_mine * (q_run / (1.0 - p_run)) + q_mine
        if sweep == SWEEPS - 1:
            arrived = crecv[sweep, lax.rem(cut + n_cut - 1, n_cut), 1, :tiles]
            spread[:tiles, :] = arrived
            for t in range(edge, tiles - edge):
                at = (t - edge) * LANES
                def_ref[0:1, at:at + LANES] = spread[t:t + 1, :] - states[0:1, t * LANES:(t + 1) * LANES]
                new_ref[0:1, at:at + LANES] = new[t:t + 1, :]
        else:
            spread[:tiles, :] = new
            states = jnp.concatenate(
                [jnp.broadcast_to(spread[t:t + 1, :], (ROWS, LANES)) for t in range(tiles)], axis=1)


def shards(sizes, couplings, edge_mask, slice_mass, sources, slice_states):
    n_mesh, n_sub, n_cut = sizes
    n_sec = n_mesh * n_sub
    blocks = couplings.shape[0]
    wide = blocks * BLOCK + 2 * HALO
    tiles = wide // LANES
    lines = -(-tiles // ROWS) * ROWS
    steps = sources.shape[1]
    vrows = -(-(2 + steps) // ROWS) * ROWS
    f32 = jnp.float32
    vmem = pl.BlockSpec(memory_space=pltpu.VMEM)
    out = jax.ShapeDtypeStruct(slice_states.shape, f32)
    return pl.pallas_call(
        functools.partial(kernel, sizes),
        out_shape=(out, out),
        in_specs=[pl.BlockSpec(memory_space=pl.ANY), pl.BlockSpec(memory_space=pltpu.SMEM), vmem, vmem, vmem],
        out_specs=(vmem, vmem),
        scratch_shapes=[
            pltpu.VMEM((blocks // 2 + 4, 8 * BLOCK, 2 * LANES), jnp.bfloat16),
            pltpu.VMEM((blocks + BEFORE + REACH + 1, BLOCK, 4 * BLOCK), f32),
            pltpu.VMEM((blocks + BEFORE + REACH + 1, 2, LANES), f32),
            pltpu.VMEM((2, vrows, HALO), f32),
            pltpu.VMEM((2, vrows, HALO), f32),
            pltpu.VMEM((ROWS, LANES), f32),
            pltpu.VMEM((n_sec - 1, ROWS, LANES), f32),
            pltpu.VMEM((2, 2, 2 * ROWS, LANES), f32),
            pltpu.VMEM((2, n_sec - 1, 2 * ROWS, LANES), f32),
            pltpu.VMEM((SWEEPS, 2, lines, LANES), f32),
            pltpu.VMEM((SWEEPS, n_cut, 2, lines, LANES), f32),
            pltpu.VMEM((lines, LANES), f32),
            pltpu.SemaphoreType.DMA,
            pltpu.SemaphoreType.DMA((6,)),
            pltpu.SemaphoreType.DMA((4,)),
            pltpu.SemaphoreType.DMA((4,)),
            pltpu.SemaphoreType.DMA((n_sec - 1,)),
            pltpu.SemaphoreType.DMA((n_sec - 1,)),
            pltpu.SemaphoreType.DMA((2, n_sec - 1)),
            pltpu.SemaphoreType.DMA((2, n_sec - 1)),
            pltpu.SemaphoreType.DMA((SWEEPS, n_cut - 1)),
            pltpu.SemaphoreType.DMA((SWEEPS, n_cut - 1)),
        ],
        compiler_params=pltpu.CompilerParams(
            collective_id=0, has_side_effects=True, vmem_limit_bytes=32 * 1024 * 1024),
    )(couplings, edge_mask.T, slice_mass, sources, slice_states)


def solution(mesh):
    rows = P(("groups", "cuts"), ("mesh", "sub"))
    placed = (
        P(("mesh", "sub"), None, None),
        P(("mesh", "sub"), None),
        rows,
        P(("groups", "cuts"), None, ("mesh", "sub")),
        rows,
    )
    sizes = (mesh.shape["mesh"], mesh.shape["sub"], mesh.shape["cuts"])
    return jax.shard_map(
        functools.partial(shards, sizes),
        mesh=mesh,
        in_specs=placed,
        out_specs=(rows, rows),
        check_vma=False,
    )
```

time: 71.9 us -> 57.5 us (0.80)
  Pallas kernels: 66.4 us -> 51.4 us
    pallas_call x1, Pallas kernels: 66.4 us -> 51.4 us  [shards(): pl.pallas_call(functools.partial(kernel, sizes), out_shape=(out, out), in...]
    unnamed x11 -> x12, local copies, waits for them, and re-layouts: 4.55 us -> 5.16 us
where the time goes in v1:
time: 57.5 us; the launch traced here: 57.2 us
  Pallas kernels  51.4 us (89%)
  local copies, waits for them, and re-layouts  5.16 us (9%)
  between operations  0.65 us (1%)
    pallas_call x1, Pallas kernels, shards(): pl.pallas_call(functools.partial(kernel, sizes), out_shape=(out, out), in...  51.4 us
    unnamed x12, local copies, waits for them, and re-layouts  5.16 us

profile of v1, /device:TPU:0, one launch (start us, length us, event | category | flops | bytes accessed | tf_op | source)
XLA Modules:
  0.0 57.2 jit_solution(252714909322850889)
XLA Ops:
  0.6 0.0 copy-start
  0.6 1.2 %copy-done = f32[16,64,256]{2,1,0:T(8,128)S(1)} copy-done((f32[16,64,256]{2,1,0:T(8,128)S(1)}, f32[16,64,256]{2,1,0:T(8,128)}, u32[]{:S(2)}) %copy-start) | copy-done | bytes 1048600
  1.9 0.0 copy-start.1
  1.9 0.7 %copy-done.1 = f32[1,2,1024]{2,1,0:T(2,128)S(1)} copy-done((f32[1,2,1024]{2,1,0:T(2,128)S(1)}, f32[1,2,1024]{2,1,0:T(2,128)}, u32[]{:S(2)}) %copy-start.1) | copy-done | bytes 8216
  2.6 0.0 copy-start.2
  2.6 0.7 %copy-done.2 = f32[1,1024]{1,0:T(1,128)S(1)} copy-done((f32[1,1024]{1,0:T(1,128)S(1)}, f32[1,1024]{1,0:T(1,128)}, u32[]{:S(2)}) %copy-start.2) | copy-done | bytes 4120
  3.2 0.0 copy-start.3
  3.2 0.7 %copy-done.3 = f32[1,1024]{1,0:T(1,128)S(1)} copy-done((f32[1,1024]{1,0:T(1,128)S(1)}, f32[1,1024]{1,0:T(1,128)}, u32[]{:S(2)}) %copy-start.3) | copy-done | bytes 4120
  3.9 0.0 copy-start.4
  3.9 0.7 %copy-done.4 = s32[16,3]{0,1:T(4,128)S(1)} copy-done((s32[16,3]{0,1:T(4,128)S(1)}, s32[16,3]{0,1:T(4,128)}, u32[]{:S(2)}) %copy-start.4) | copy-done | bytes 216
  4.6 51.4 %shard_map.68 = (f32[1,1024]{1,0:T(1,128)S(1)}, f32[1,1024]{1,0:T(1,128)S(1)}) custom-call(f32[16,64,256]{2,1,0:T(8,128)S(1)} %copy-done, s32[3,16]{1,0:T(4,128)S(1)} %bitcast.1, f32[1,1024]{1,0:T(1,128)S(1)} %copy-done.2, f32[1,2,1024]{2,1,0:T(2,128)S(1)} %copy-done.1, f32[1,1024]{1,0:T(1,128)S(1)} %copy-done.3), custom_call_target="tpu_custom_call" | custom-call | tf_op jit(solution)/shard_map/pallas_call | solution.py:363
  56.0 0.6 %copy.9 = f32[1,1024]{1,0:T(1,128)} copy(f32[1,1024]{1,0:T(1,128)S(1)} %get-tuple-element.4) | data formatting | bytes 8192
  56.6 0.6 %copy.10 = f32[1,1024]{1,0:T(1,128)} copy(f32[1,1024]{1,0:T(1,128)S(1)} %get-tuple-element.5) | data formatting | bytes 8192
Async XLA Ops:
  0.6 1.2 %copy-start = (f32[16,64,256]{2,1,0:T(8,128)S(1)}, f32[16,64,256]{2,1,0:T(8,128)}, u32[]{:S(2)}) copy-start(f32[16,64,256]{2,1,0:T(8,128)} %coup.1) | copy-start | bytes 3145732
  1.9 0.7 %copy-start.1 = (f32[1,2,1024]{2,1,0:T(2,128)S(1)}, f32[1,2,1024]{2,1,0:T(2,128)}, u32[]{:S(2)}) copy-start(f32[1,2,1024]{2,1,0:T(2,128)} %src_ref.1) | copy-start | bytes 24580
  2.6 0.7 %copy-start.2 = (f32[1,1024]{1,0:T(1,128)S(1)}, f32[1,1024]{1,0:T(1,128)}, u32[]{:S(2)}) copy-start(f32[1,1024]{1,0:T(1,128)} %mass_ref.1) | copy-start | bytes 12292
  3.2 0.7 %copy-start.3 = (f32[1,1024]{1,0:T(1,128)S(1)}, f32[1,1024]{1,0:T(1,128)}, u32[]{:S(2)}) copy-start(f32[1,1024]{1,0:T(1,128)} %st_ref.1) | copy-start | bytes 12292
  3.9 0.7 %copy-start.4 = (s32[16,3]{0,1:T(4,128)S(1)}, s32[16,3]{0,1:T(4,128)}, u32[]{:S(2)}) copy-start(s32[16,3]{0,1:T(4,128)} %param.6) | copy-start | bytes 580

commit v2 on v1

--- a/solution.py
+++ b/solution.py
@@ -18,9 +18,9 @@
 MESH = pl.DeviceIdType.MESH
 
 
-def kernel(sizes, coup, mask, mass_ref, src_ref, st_ref, new_ref, def_ref,
-           W, ext, fac, vsend, vrecv, tsend, trecv, send, recv, csend, crecv, spread,
-           lsem, hsem, fsem, vsem, ts_sem, tr_sem, xs_sem, xr_sem, cs_sem, cr_sem):
+def kernel(sizes, coup, mask, mass_in, src_in, st_in, new_out, def_out,
+           mass_ref, src_ref, st_ref, new_ref, def_ref, W, ext, fac, vsend, vrecv, tsend, trecv, send, recv, csend, crecv, spread,
+           isem, lsem, hsem, fsem, vsem, ts_sem, tr_sem, xs_sem, xr_sem, cs_sem, cr_sem):
     n_mesh, n_sub, n_cut = sizes
     n_sec = n_mesh * n_sub
     blocks = coup.shape[0]
@@ -29,7 +29,7 @@
     wide = local + 2 * HALO
     tiles = wide // LANES
     edge = HALO // LANES
-    steps = src_ref.shape[1]
+    steps = src_in.shape[1]
 
     sector = lax.axis_index("mesh") * n_sub + lax.axis_index("sub")
     cut = lax.axis_index("cuts")
@@ -47,6 +47,10 @@
     for d in range(1, n_cut):
         pl.semaphore_signal(barrier, inc=1, device_id=cut_id(d), device_id_type=MESH)
     fetch = pltpu.make_async_copy(coup, ext.at[BEFORE:BEFORE + blocks], lsem)
+    small = [pltpu.make_async_copy(a, b, isem.at[i]) for i, (a, b) in enumerate(
+        ((mass_in, mass_ref), (src_in, src_ref), (st_in, st_ref)))]
+    for copy in small:
+        copy.start()
     fetch.start()
 
     low_half = lax.broadcasted_iota(jnp.int32, (BLOCK, LANES), 1) < BLOCK
@@ -65,6 +69,8 @@
     ext[last, :, LANES:] = zero
     for b in range(2):
         ext[b, :, :LANES] = zero
+    for copy in small:
+        copy.wait()
     for i, at in enumerate((local - HALO, 0)):
         vsend[i, 0:1, :] = mass_ref[0:1, at:at + HALO]
         vsend[i, 1:2, :] = st_ref[0:1, at:at + HALO]
@@ -342,6 +348,12 @@
                 at = (t - edge) * LANES
                 def_ref[0:1, at:at + LANES] = spread[t:t + 1, :] - states[0:1, t * LANES:(t + 1) * LANES]
                 new_ref[0:1, at:at + LANES] = new[t:t + 1, :]
+            ends = [pltpu.make_async_copy(a, b, isem.at[3 + i]) for i, (a, b) in enumerate(
+                ((new_ref, new_out), (def_ref, def_out)))]
+            for copy in ends:
+                copy.start()
+            for copy in ends:
+                copy.wait()
         else:
             spread[:tiles, :] = new
             states = jnp.concatenate(
@@ -358,14 +370,19 @@
     steps = sources.shape[1]
     vrows = -(-(2 + steps) // ROWS) * ROWS
     f32 = jnp.float32
-    vmem = pl.BlockSpec(memory_space=pltpu.VMEM)
+    hbm = pl.BlockSpec(memory_space=pltpu.HBM)
     out = jax.ShapeDtypeStruct(slice_states.shape, f32)
     return pl.pallas_call(
         functools.partial(kernel, sizes),
         out_shape=(out, out),
-        in_specs=[pl.BlockSpec(memory_space=pl.ANY), pl.BlockSpec(memory_space=pltpu.SMEM), vmem, vmem, vmem],
-        out_specs=(vmem, vmem),
+        in_specs=[hbm, pl.BlockSpec(memory_space=pltpu.SMEM), hbm, hbm, hbm],
+        out_specs=(hbm, hbm),
         scratch_shapes=[
+            pltpu.VMEM(slice_mass.shape, f32),
+            pltpu.VMEM(sources.shape, f32),
+            pltpu.VMEM(slice_states.shape, f32),
+            pltpu.VMEM(slice_states.shape, f32),
+            pltpu.VMEM(slice_states.shape, f32),
             pltpu.VMEM((blocks // 2 + 4, 8 * BLOCK, 2 * LANES), jnp.bfloat16),
             pltpu.VMEM((blocks + BEFORE + REACH + 1, BLOCK, 4 * BLOCK), f32),
             pltpu.VMEM((blocks + BEFORE + REACH + 1, 2, LANES), f32),
@@ -378,6 +395,7 @@
             pltpu.VMEM((SWEEPS, 2, lines, LANES), f32),
             pltpu.VMEM((SWEEPS, n_cut, 2, lines, LANES), f32),
             pltpu.VMEM((lines, LANES), f32),
+            pltpu.SemaphoreType.DMA((5,)),
             pltpu.SemaphoreType.DMA,
             pltpu.SemaphoreType.DMA((6,)),
             pltpu.SemaphoreType.DMA((4,)),
@@ -390,7 +408,7 @@
             pltpu.SemaphoreType.DMA((SWEEPS, n_cut - 1)),
         ],
         compiler_params=pltpu.CompilerParams(
-            collective_id=0, has_side_effects=True, vmem_limit_bytes=32 * 1024 * 1024),
+            collective_id=0, has_side_effects=True, vmem_limit_bytes=62 * 1024 * 1024),
     )(couplings, edge_mask.T, slice_mass, sources, slice_states)
 
 

time: 57.5 us -> 54.9 us (0.955)
  local copies, waits for them, and re-layouts: 5.16 us -> 1.86 us
  Pallas kernels: 51.4 us -> 52.2 us
    unnamed x12 -> x4, local copies, waits for them, and re-layouts: 5.16 us -> 1.86 us
    pallas_call x1, Pallas kernels: 51.4 us -> 52.2 us  [shards(): pl.pallas_call(functools.partial(kernel, sizes), out_shape=(out, out), in...]
where the time goes in v2:
time: 54.9 us; the launch traced here: 54.7 us
  Pallas kernels  52.2 us (95%)
  local copies, waits for them, and re-layouts  1.86 us (3%)
  between operations  0.65 us (1%)
    pallas_call x1, Pallas kernels, shards(): pl.pallas_call(functools.partial(kernel, sizes), out_shape=(out, out), in...  52.2 us
    unnamed x4, local copies, waits for them, and re-layouts  1.86 us

profile of v2, /device:TPU:0, one launch (start us, length us, event | category | flops | bytes accessed | tf_op | source)
XLA Modules:
  0.0 54.7 jit_solution(12851546668395440691)
XLA Ops:
  0.6 52.2 %shard_map.68 = (f32[1,1024]{1,0:T(1,128)}, f32[1,1024]{1,0:T(1,128)}) custom-call(f32[16,64,256]{2,1,0:T(8,128)} %coup.1, s32[3,16]{1,0:T(4,128)} %bitcast.1, f32[1,1024]{1,0:T(1,128)} %mass_in.1, f32[1,2,1024]{2,1,0:T(2,128)} %src_in.1, f32[1,1024]{1,0:T(1,128)} %st_in.1), custom_call_target="tpu_custom_call" | custom-call | tf_op jit(solution)/shard_map/pallas_call | solution.py:375
  52.8 0.0 copy-start
  52.8 1.3 %copy.9 = f32[1,1024]{1,0:T(1,128)} copy(f32[1,1024]{1,0:T(1,128)} %get-tuple-element.4) | data formatting | bytes 8192
  54.1 0.0 copy-done
  54.1 0.6 %copy.10 = f32[1,1024]{1,0:T(1,128)} copy(f32[1,1024]{1,0:T(1,128)S(1)} %copy-done) | data formatting | bytes 8192
Async XLA Ops:
  52.8 1.3 %copy-start = (f32[1,1024]{1,0:T(1,128)S(1)}, f32[1,1024]{1,0:T(1,128)}, u32[]{:S(2)}) copy-start(f32[1,1024]{1,0:T(1,128)} %get-tuple-element.5) | copy-start | bytes 12292

commit v3 on v2

--- a/solution.py
+++ b/solution.py
@@ -18,8 +18,8 @@
 MESH = pl.DeviceIdType.MESH
 
 
-def kernel(sizes, coup, mask, mass_in, src_in, st_in, new_out, def_out,
-           mass_ref, src_ref, st_ref, new_ref, def_ref, W, ext, fac, vsend, vrecv, tsend, trecv, send, recv, csend, crecv, spread,
+def kernel(sizes, coup, mask, mass_in, src_in, st_in, both_ref,
+           mass_ref, src_ref, st_ref, W, ext, fac, vsend, vrecv, tsend, trecv, send, recv, csend, crecv, spread,
            isem, lsem, hsem, fsem, vsem, ts_sem, tr_sem, xs_sem, xr_sem, cs_sem, cr_sem):
     n_mesh, n_sub, n_cut = sizes
     n_sec = n_mesh * n_sub
@@ -30,6 +30,7 @@
     tiles = wide // LANES
     edge = HALO // LANES
     steps = src_in.shape[1]
+    new_ref, def_ref = both_ref.at[0], both_ref.at[1]
 
     sector = lax.axis_index("mesh") * n_sub + lax.axis_index("sub")
     cut = lax.axis_index("cuts")
@@ -107,7 +108,7 @@
         first.append(pltpu.make_async_remote_copy(
             tsend, trecv.at[d - 1], ts_sem.at[d - 1], tr_sem.at[d - 1],
             device_id=sector_id(d), device_id_type=MESH))
-    for copy in first[3:] + first[:3]:
+    for copy in first:
         copy.start()
 
     def turned(x):
@@ -348,12 +349,6 @@
                 at = (t - edge) * LANES
                 def_ref[0:1, at:at + LANES] = spread[t:t + 1, :] - states[0:1, t * LANES:(t + 1) * LANES]
                 new_ref[0:1, at:at + LANES] = new[t:t + 1, :]
-            ends = [pltpu.make_async_copy(a, b, isem.at[3 + i]) for i, (a, b) in enumerate(
-                ((new_ref, new_out), (def_ref, def_out)))]
-            for copy in ends:
-                copy.start()
-            for copy in ends:
-                copy.wait()
         else:
             spread[:tiles, :] = new
             states = jnp.concatenate(
@@ -370,18 +365,17 @@
     steps = sources.shape[1]
     vrows = -(-(2 + steps) // ROWS) * ROWS
     f32 = jnp.float32
+    vmem = pl.BlockSpec(memory_space=pltpu.VMEM)
     hbm = pl.BlockSpec(memory_space=pltpu.HBM)
-    out = jax.ShapeDtypeStruct(slice_states.shape, f32)
-    return pl.pallas_call(
+    out = jax.ShapeDtypeStruct((2,) + slice_states.shape, f32)
+    both = pl.pallas_call(
         functools.partial(kernel, sizes),
-        out_shape=(out, out),
+        out_shape=out,
         in_specs=[hbm, pl.BlockSpec(memory_space=pltpu.SMEM), hbm, hbm, hbm],
-        out_specs=(hbm, hbm),
+        out_specs=vmem,
         scratch_shapes=[
             pltpu.VMEM(slice_mass.shape, f32),
             pltpu.VMEM(sources.shape, f32),
-            pltpu.VMEM(slice_states.shape, f32),
-            pltpu.VMEM(slice_states.shape, f32),
             pltpu.VMEM(slice_states.shape, f32),
             pltpu.VMEM((blocks // 2 + 4, 8 * BLOCK, 2 * LANES), jnp.bfloat16),
             pltpu.VMEM((blocks + BEFORE + REACH + 1, BLOCK, 4 * BLOCK), f32),
@@ -395,7 +389,7 @@
             pltpu.VMEM((SWEEPS, 2, lines, LANES), f32),
             pltpu.VMEM((SWEEPS, n_cut, 2, lines, LANES), f32),
             pltpu.VMEM((lines, LANES), f32),
-            pltpu.SemaphoreType.DMA((5,)),
+            pltpu.SemaphoreType.DMA((3,)),
             pltpu.SemaphoreType.DMA,
             pltpu.SemaphoreType.DMA((6,)),
             pltpu.SemaphoreType.DMA((4,)),
@@ -410,6 +404,7 @@
         compiler_params=pltpu.CompilerParams(
             collective_id=0, has_side_effects=True, vmem_limit_bytes=62 * 1024 * 1024),
     )(couplings, edge_mask.T, slice_mass, sources, slice_states)
+    return both[0], both[1]
 
 
 def solution(mesh):

time: 54.9 us -> 54.5 us (level)
  local copies, waits for them, and re-layouts: 1.86 us -> 1.28 us
    unnamed x4 -> x0, local copies, waits for them, and re-layouts: 1.86 us -> none
    squeeze x0 -> x1, local copies, waits for them, and re-layouts: none -> 1.28 us  [shards(): return (both[0], both[1])]
where the time goes in v3:
time: 54.5 us; the launch traced here: 54.2 us
  Pallas kernels  52.3 us (96%)
  local copies, waits for them, and re-layouts  1.28 us (2%)
  between operations  0.64 us (1%)
    pallas_call x1, Pallas kernels, shards(): pl.pallas_call(functools.partial(kernel, sizes), out_shape=out, in_specs=...  52.3 us
    squeeze x1, local copies, waits for them, and re-layouts, shards(): return (both[0], both[1])  1.28 us

profile of v3, /device:TPU:0, one launch (start us, length us, event | category | flops | bytes accessed | tf_op | source)
XLA Modules:
  0.0 54.2 jit_solution(8144490381279445528)
XLA Ops:
  0.6 52.3 %shard_map.68 = f32[2,1,1024]{2,1,0:T(1,128)} custom-call(f32[16,64,256]{2,1,0:T(8,128)} %coup.1, s32[3,16]{1,0:T(4,128)} %bitcast.5, f32[1,1024]{1,0:T(1,128)} %mass_in.1, f32[1,2,1024]{2,1,0:T(2,128)} %src_in.1, f32[1,1024]{1,0:T(1,128)} %st_in.1), custom_call_target="tpu_custom_call" | custom-call | tf_op jit(solution)/shard_map/pallas_call | solution.py:371
  52.9 1.3 %slice_bitcast_fusion = (f32[1,1024]{1,0:T(1,128)}, f32[1,1024]{1,0:T(1,128)}) fusion(f32[2,1,1024]{2,1,0:T(1,128)} %shard_map.68), kind=kLoop, calls=%fused_computation | loop fusion | bytes 16384 | tf_op jit(solution)/shard_map/squeeze | solution.py:407
